TPU v7x, 512 devices: a whole 4x4x16 slice. The times are simulated.
512 devices in a mesh: outer: 32 (over y, x, z_hi), inner: 16 (over z_lo, core).
Axes of the slice: x: 4, y: 4, z: 16 (z_hi: 2, z_lo: 8; z = z_hi * 8 + z_lo), core: 2. Of those that a mesh axis runs over, the one named last changes fastest.
Arguments:
- picture_embeddings: bfloat16 [65536, 1536], P(('outer', 'inner')), may hold values from -0.15625 to 0.15625
- text_emb: bfloat16 [65536, 1536], P(('outer', 'inner')), may hold values from -0.15625 to 0.15625
- positive: int32 [65536], P(('outer', 'inner')), may hold values from 0 to 65535, as said below
- ln_inverse_heat: float32 [1], replicated, may hold values from 1.6 to 3
- logit_bias: float32 [1], replicated, may hold values from -5 to -1
Outputs:
- image_grad: float32 [65536, 1536], P(('outer', 'inner'))
- text_grad: float32 [65536, 1536], P(('outer', 'inner'))
Inputs may be any that keep to these rules, and one draw needn't show every extreme that they name: `positive`: positive_i lies in block (g + 1) mod 32 of 2048 rows, where g is the block of row i, and every text row is named by exactly one image row.
All inputs are finite; a program needn't handle non-finite values.
Results may differ from a plain program's by a relative error of at most 0.0032.
Values may be sent and summed in bfloat16 or wider, within the bound.
A program may use at most 64 MiB of HBM per device.

v0:
```python
import jax
import jax.numpy as jnp
from jax import lax
from jax.sharding import PartitionSpec as P


def from_behind(value, axis, steps):
    count = lax.axis_size(axis)
    pairs = [(source, (source + steps) % count) for source in range(count)]
    return lax.ppermute(value, axis, pairs)


def similarity_grid(first_factor, second_factor, inverse_heat, group_start_index):
    return (
        inverse_heat
        * lax.dot_general(
            first_factor,
            second_factor,
            (((1,), (1,)), ((), ())),
            preferred_element_type=jnp.float32,
        )
        + group_start_index
    )


def gradient_coefficients(scaled_similarity, diagonal_indicator, inverse_heat, number_entries):
    plus_minus_truth = jnp.where(diagonal_indicator, 1.0, -1.0).astype(jnp.float32)
    return (
        -plus_minus_truth
        * inverse_heat
        * jax.nn.sigmoid(-plus_minus_truth * scaled_similarity)
        / number_entries
    ).astype(jnp.bfloat16)


def per_device(picture_embeddings, text_emb, positive, ln_inverse_heat, logit_bias):
    inverse_heat = jnp.exp(ln_inverse_heat[0])
    group_start_index = logit_bias[0]
    number_entries = picture_embeddings.shape[0]
    group_rows = number_entries * lax.axis_size("inner")
    target_labels = positive % group_rows
    visiting = from_behind(text_emb, "outer", -1)
    extracted_piece = lax.all_gather(visiting, "inner", axis=0, tiled=True)
    row_positions = lax.iota(jnp.int32, extracted_piece.shape[0])
    scaled_similarity = similarity_grid(
        picture_embeddings, extracted_piece, inverse_heat, group_start_index
    )
    coefficient_table = gradient_coefficients(
        scaled_similarity,
        target_labels[:, None] == row_positions[None, :],
        inverse_heat,
        number_entries,
    )
    grad_sum = jnp.dot(coefficient_table, extracted_piece, preferred_element_type=jnp.float32)
    weight_rows = coefficient_table
    image_grad, weight_rows = (grad_sum, weight_rows)
    swapped = lax.all_to_all(weight_rows, "inner", split_axis=1, concat_axis=0, tiled=True)
    partial_value = lax.dot_general(
        swapped,
        lax.all_gather(picture_embeddings, "inner", axis=0, tiled=True),
        (((0,), (0,)), ((), ())),
        preferred_element_type=jnp.float32,
    )
    text_grad = from_behind(partial_value, "outer", 1)
    return (image_grad, text_grad)


def solution(mesh):
    return jax.shard_map(
        per_device,
        mesh=mesh,
        in_specs=(
            P(("outer", "inner"), None),
            P(("outer", "inner"), None),
            P(("outer", "inner")),
            P(),
            P(),
        ),
        out_specs=(P(("outer", "inner"), None), P(("outer", "inner"), None)),
        check_vma=False,
    )
```

profile of v0, /device:TPU:1, one launch (start us, length us, event | category | flops | bytes accessed | tf_op | source)
XLA Modules:
  0.0 377.9 jit_solution(16916505107846638729)
XLA Ops:
  7.2 0.0 all-gather.3.cloned.1.call-start
  7.2 20.9 %collective-permute-start = (bf16[128,1536]{1,0:T(8,128)(2,1)}, bf16[128,1536]{1,0:T(8,128)(2,1)S(1)}, u32[]{:S(2)}, u32[]{:S(2)}) collective-permute-start(bf16[128,1536]{1,0:T(8,128)(2,1)} %param.6), channel_id=1, source_target_pairs={{0,496},{16,0},{32,16},{48,32},{64,48},{80,64},{96,80},{112,96},{1... | collective-permute-start | bytes 1179656 | tf_op jit(solution)/shard_map/ppermute | solution.py:10
  28.1 31.5 %collective-permute-done = bf16[128,1536]{1,0:T(8,128)(2,1)S(1)} collective-permute-done((bf16[128,1536]{1,0:T(8,128)(2,1)}, bf16[128,1536]{1,0:T(8,128)(2,1)S(1)}, u32[]{:S(2)}, u32[]{:S(2)}) %collective-permute-start) | collective-permute-done | bytes 393248 | tf_op jit(solution)/shard_map/ppermute | solution.py:10
  59.7 0.0 copy-start
  59.7 0.7 copy-done
  60.4 0.0 all-gather.3.cloned.1.call-update
  60.4 0.0 all-gather.5.cloned.1.call-start
  60.5 0.7 all-gather.5.cloned.1.call-update
  62.5 0.7 and_select_fusion
  63.2 107.5 %all-gather.3.cloned.1.call-done = bf16[2048,1536]{1,0:T(8,128)(2,1)} async-done(((bf16[128,1536]{1,0:T(8,128)(2,1)}), bf16[2048,1536]{1,0:T(8,128)(2,1)}) %all-gather.3.cloned.1.call-update) | async-done | bytes 6291472 | tf_op jit(solution)/shard_map/all_gather | solution.py:43
  170.7 5.2 %fusion.8 = bf16[128,2048]{1,0:T(8,128)(2,1)S(1)} fusion(bf16[128,1536]{1,0:T(8,128)(2,1)} %param.5, bf16[2048,1536]{1,0:T(8,128)(2,1)} %all-gather.3.cloned.1.call-done, f32[]{:T(128)} %bitcast.16, f32[]{:T(128)} %bitcast, s32[128]{0:T(128)S(1)} %and_select_fusion), kind=kOutput, calls=%fused_computation.9 | convolution fusion | flops 808714240 | bytes 7209480 | tf_op jit(solution)/shard_map/dot_general | solution.py:16
  175.9 0.9 copy_bitcast_fusion
  176.9 0.0 slice-start
  176.9 10.8 %all-to-all-start = ((bf16[128,16,128]{2,0,1:T(8,128)(2,1)}), bf16[128,16,128]{2,0,1:T(8,128)(2,1)S(1)}, u32[]{:S(2)}, u32[]{:S(2)}) async-start(bf16[128,16,128]{2,0,1:T(8,128)(2,1)} %copy_bitcast_fusion), calls=%async_computation | async-start | bytes 1048576 | tf_op jit(solution)/shard_map/all_to_all | solution.py:57
  187.7 100.0 %all-gather.5.cloned.1.call-done = bf16[2048,1536]{1,0:T(8,128)(2,1)} async-done(((bf16[128,1536]{1,0:T(8,128)(2,1)}), bf16[2048,1536]{1,0:T(8,128)(2,1)}) %all-gather.5.cloned.1.call-update) | async-done | bytes 6291472 | tf_op jit(solution)/shard_map/all_gather | solution.py:60
  287.7 0.0 all-to-all-done
  287.7 0.0 slice-start.1
  287.7 3.9 %fusion.11 = f32[128,1536]{1,0:T(8,128)S(1)} fusion(bf16[2048,128]{1,0:T(8,128)(2,1)S(1)} %bitcast.19, bf16[2048,1536]{1,0:T(8,128)(2,1)} %all-gather.5.cloned.1.call-done), kind=kOutput, calls=%fused_computation.17 | convolution fusion | flops 805306368 | bytes 7602176 | tf_op jit(solution)/shard_map/dot_general | solution.py:58
  291.6 6.0 %collective-permute-start.1 = (f32[128,1536]{1,0:T(8,128)S(1)}, f32[128,1536]{1,0:T(8,128)S(1)}, u32[]{:S(2)}, u32[]{:S(2)}) collective-permute-start(f32[128,1536]{1,0:T(8,128)S(1)} %fusion.11), channel_id=1, source_target_pairs={{0,16},{16,32},{32,48},{48,64},{64,80},{80,96},{96,112},{112,128},... | collective-permute-start | bytes 2359304 | tf_op jit(solution)/shard_map/ppermute | solution.py:10
  297.6 0.0 slice-done
  297.6 0.0 slice-done.1
  297.6 1.9 fusion.10
  299.5 70.7 %collective-permute-done.1 = f32[128,1536]{1,0:T(8,128)S(1)} collective-permute-done((f32[128,1536]{1,0:T(8,128)S(1)}, f32[128,1536]{1,0:T(8,128)S(1)}, u32[]{:S(2)}, u32[]{:S(2)}) %collective-permute-start.1) | collective-permute-done | bytes 786464 | tf_op jit(solution)/shard_map/ppermute | solution.py:10
  370.2 0.9 copy.13
  (1 shorter events, 0.0 us)
Async XLA Ops:
  7.2 163.6 %all-gather.3.cloned.1.call-start = ((), (), s32[]{:S(2)}) async-start(), calls=%async_computation.1 | async-start | bytes 6684672 | tf_op jit(solution)/shard_map/all_gather | solution.py:43
  7.2 52.5 %collective-permute-start = (bf16[128,1536]{1,0:T(8,128)(2,1)}, bf16[128,1536]{1,0:T(8,128)(2,1)S(1)}, u32[]{:S(2)}, u32[]{:S(2)}) collective-permute-start(bf16[128,1536]{1,0:T(8,128)(2,1)} %param.6), channel_id=1, source_target_pairs={{0,496},{16,0},{32,16},{48,32},{64,48},{80,64},{96,80},{112,96},{1... | collective-permute-start | bytes 1179656 | tf_op jit(solution)/shard_map/ppermute | solution.py:10
  59.7 0.7 copy-start
  60.4 227.2 %all-gather.5.cloned.1.call-start = ((), (), s32[]{:S(2)}) async-start(), calls=%async_computation.2 | async-start | bytes 6684672 | tf_op jit(solution)/shard_map/all_gather | solution.py:60
  176.9 120.7 %slice-start = ((s8[6291456]{0:T(1024)(128)(4,1)}), s8[2097152]{0:T(1024)(128)(4,1)S(1)}, s32[]{:S(2)}) async-start(s8[6291456]{0:T(1024)(128)(4,1)} %bitcast.17), calls=%async_computation.3 | async-start | bytes 4194304
  176.9 110.8 %all-to-all-start = ((bf16[128,16,128]{2,0,1:T(8,128)(2,1)}), bf16[128,16,128]{2,0,1:T(8,128)(2,1)S(1)}, u32[]{:S(2)}, u32[]{:S(2)}) async-start(bf16[128,16,128]{2,0,1:T(8,128)(2,1)} %copy_bitcast_fusion), calls=%async_computation | async-start | bytes 1048576 | tf_op jit(solution)/shard_map/all_to_all | solution.py:57
  287.7 10.0 %slice-start.1 = ((s8[6291456]{0:T(1024)(128)(4,1)}), s8[4194304]{0:T(1024)(128)(4,1)S(1)}, s32[]{:S(2)}) async-start(s8[6291456]{0:T(1024)(128)(4,1)} %bitcast.17), calls=%async_computation.4 | async-start | bytes 8388608
  291.6 78.6 %collective-permute-start.1 = (f32[128,1536]{1,0:T(8,128)S(1)}, f32[128,1536]{1,0:T(8,128)S(1)}, u32[]{:S(2)}, u32[]{:S(2)}) collective-permute-start(f32[128,1536]{1,0:T(8,128)S(1)} %fusion.11), channel_id=1, source_target_pairs={{0,16},{16,32},{32,48},{48,64},{64,80},{80,96},{96,112},{112,128},... | collective-permute-start | bytes 2359304 | tf_op jit(solution)/shard_map/ppermute | solution.py:10
Sparse Core Ops, SparseCore 0:
  60.6 110.1 all-gather.2
  172.8 114.8 all-gather.4
where the time goes:
time: 378 us
  waiting for transfers between devices  310 us (82%)
  starting transfers between devices  37.8 us (10%)
  between operations  15.4 us (4%)
  matrix products  11 us (3%)
    all_gather x1, waiting for transfers between devices, per_device(): extracted_piece = lax.all_gather(visiting, 'inner', axis=0, tiled=True)  108 us
    ppermute x2, waiting for transfers between devices, from_behind(): return lax.ppermute(value, axis, pairs)  102 us
    all_gather x1, waiting for transfers between devices, per_device(): lax.all_gather(picture_embeddings, 'inner', axis=0, tiled=True)  100 us
    ppermute x2, starting transfers between devices, from_behind(): return lax.ppermute(value, axis, pairs)  26.9 us
    all_to_all x1, starting transfers between devices, per_device(): lax.all_to_all(weight_rows, 'inner', split_axis=1, concat_axis=0, tiled=T...  10.8 us
  transfers between devices with their start and end apart: 5, of which 4 were waited for; matrix products, arithmetic and copies ran while one was open for 2% of the time, Pallas kernels for 0%

commit v1 on v0

v1 whole, which is shorter than its diff:
```python
import jax
import jax.numpy as jnp
from jax import lax
from jax.experimental import pallas as pl
from jax.experimental.pallas import tpu as pltpu
from jax.sharding import PartitionSpec as P

X = 4
LEVELS = 16
PIECE = 32
ROWS = 128
CHUNK = 256
MESH = pl.DeviceIdType.MESH


def offset_of(step):
    return ((step + 1) // 2) * (2 * (step % 2) - 1)


def device(column, z, core):
    return (2 * column + z // 8, (z % 8) * 2 + core)


def rows(index, size=PIECE):
    return pl.ds(pl.multiple_of(index * size, size), size)


def kernel(
    heat_ref, bias_ref, image_ref, text_ref, positive_ref,
    image_out, text_out,
    relay, stream, own, total, result, landing, places,
    f1_send, f1_recv, f2_send, f2_recv, x_send, left_recv, right_recv, far_send, far_recv,
    core_send, core_recv, y_send, y_recv, back_send, back_recv, place_send, place_recv,
):
    outer, inner = lax.axis_index("outer"), lax.axis_index("inner")
    column, z_hi = outer // 2, outer % 2
    y, x = column // X, column % X
    z_lo, core = inner // 2, inner % 2
    z = z_hi * 8 + z_lo
    patch, side = y // 2, y % 2
    half = z % 2
    group = 2 * (patch * 8 + z // 2) + half
    stream_half = jnp.where(side == 0, 1 - half, half)
    mine = x * 2 + core
    relay_half = jnp.where(side == 0, 1 - z_hi, z_hi)

    def copy(source, target, send, receive, to):
        return pltpu.make_async_remote_copy(
            src_ref=source, dst_ref=target, send_sem=send, recv_sem=receive,
            device_id=to, device_id_type=MESH,
        )

    def start(source, target, send, receive, to):
        same = (to[0] == outer) & (to[1] == inner)

        @pl.when(same)
        def _():
            pltpu.make_async_copy(source, target, receive).start()

        @pl.when(jnp.logical_not(same))
        def _():
            copy(source, target, send, receive, to).start()

    def finish(source, target, send, receive, to):
        same = (to[0] == outer) & (to[1] == inner)

        @pl.when(jnp.logical_not(same))
        def _():
            copy(source, target, send, receive, to).wait_send()

    def scatter(step, act):
        for kind, ref in ((0, image_ref), (1, text_ref)):
            his = lax.rem(outer + 32 - kind, 32) // 2
            to = (2 * ((2 * (his // 8) + 1 - kind) * X + step) + z_hi, inner)
            act(
                ref.at[rows(step)], relay.at[rows(his % 8)],
                f1_send.at[kind * X + step], f1_recv.at[his % 8], to,
            )

    @pl.loop(0, X)
    def _(step):
        scatter(step, start)

    def tell(step, act):
        q = column % 8
        target_column = (2 * patch + step // 8) * X + (step // 2) % X
        act(
            positive_ref, places.at[pl.ds(inner, 1)], place_send.at[step], place_recv,
            device(target_column, 2 * q + z_hi, step % 2),
        )

    @pl.loop(0, 16)
    def _(step):
        tell(step, start)

    def along_z(step, act, wait):
        level = (z + offset_of(step) + LEVELS) % LEVELS

        @pl.when(level % 2 == relay_half)
        def _():
            q = level // 2
            if wait:
                copy(relay.at[rows(q)], relay.at[rows(q)], f1_send.at[0], f1_recv.at[q], (outer, inner)).wait_recv()
            act(
                relay.at[rows(q)], stream.at[mine, rows(z_lo)],
                f2_send.at[q], f2_recv.at[z_lo], device(column, level, core),
            )

    @pl.loop(0, LEVELS)
    def _(step):
        along_z(step, start, True)

    to_right = (2 * (y * X + (x + 1) % X) + z_hi, inner)
    to_left = (2 * (y * X + (x + 3) % X) + z_hi, inner)
    across = (2 * ((y + 1 - 2 * side) * X + x) + z_hi, inner)
    twin = (outer, z_lo * 2 + 1 - core)
    left, right, far = (x + 3) % X, (x + 1) % X, (x + 2) % X

    def piece(slot_x, zl):
        return stream.at[slot_x * 2 + core, rows(zl)]

    def arrived(ref, receive):
        copy(ref, ref, f1_send.at[0], receive, (outer, inner)).wait_recv()

    def at_step(step, act):
        from_z = (z + offset_of(step) + LEVELS) % LEVELS

        @pl.when((step >= 0) & (step < LEVELS) & (from_z // 8 == stream_half))
        def _():
            act(from_z % 8)

    def from_level(zl):
        here = piece(x, zl)
        arrived(here, f2_recv.at[zl])
        copy(here, here, x_send.at[0], left_recv.at[zl], to_right).start()
        copy(here, here, x_send.at[1], right_recv.at[zl], to_left).start()
        copy(here, own.at[rows(zl)], y_send, y_recv, across).start()
        copy(here, here, core_send.at[x], core_recv.at[x], twin).start()

    def from_sides(zl):
        here = piece(left, zl)
        arrived(here, left_recv.at[zl])

        @pl.when(zl < 4)
        def _():
            copy(here, here, far_send.at[0], far_recv.at[zl], to_right).start()

        copy(here, here, core_send.at[left], core_recv.at[left], twin).start()
        there = piece(right, zl)
        arrived(there, right_recv.at[zl])

        @pl.when(zl >= 4)
        def _():
            copy(there, there, far_send.at[1], far_recv.at[zl], to_left).start()

        copy(there, there, core_send.at[right], core_recv.at[right], twin).start()

    def from_far(zl):
        here = piece(far, zl)
        arrived(here, far_recv.at[zl])
        copy(here, here, core_send.at[far], core_recv.at[far], twin).start()

    @pl.loop(0, LEVELS + 5)
    def _(step):
        at_step(step, from_level)
        at_step(step - 2, from_sides)
        at_step(step - 5, from_far)

    arrived(own, y_recv)
    arrived(places, place_recv)
    place = (places[...] % 2048).astype(jnp.float32)
    high = jnp.floor(place * (1.0 / 64.0))
    low = (place - 64.0 * high).astype(jnp.bfloat16)
    high = high.astype(jnp.bfloat16)

    def number(rr, slot_x, slot_core):
        return ((rr // PIECE) * 2 + slot_core) * ROWS + slot_x * PIECE + rr % PIECE

    rr = lax.broadcasted_iota(jnp.int32, (CHUNK, ROWS), 0)
    lane = lax.broadcasted_iota(jnp.int32, (CHUNK, ROWS), 1)
    pick = (lane == x * PIECE + rr % PIECE).astype(jnp.bfloat16)
    contract = (((1,), (1,)), ((), ()))
    spread = 64.0 * lax.dot_general(
        pick, high, contract, preferred_element_type=jnp.float32
    ) + lax.dot_general(pick, low, contract, preferred_element_type=jnp.float32)
    rr = lax.broadcasted_iota(jnp.int32, (CHUNK, 16), 0)
    source = lax.broadcasted_iota(jnp.int32, (CHUNK, 16), 1)
    spread = jnp.where(source == (rr // PIECE) * 2 + core, spread, 0.0)
    own_place = jnp.sum(spread, axis=1, keepdims=True)
    own_number = number(
        lax.broadcasted_iota(jnp.int32, (CHUNK, 1), 0), x, core
    ).astype(jnp.float32)
    own_key = jnp.where(side == 0, own_place, own_number)

    heat = jnp.exp(jnp.full((1, CHUNK), heat_ref[0], jnp.float32))
    bias = bias_ref[0]
    total[...] = jnp.zeros_like(total)

    @pl.loop(0, 8)
    def _(step):
        turn = step // 2
        slot_x = (x + turn + turn // 2 - 2 * (turn // 3)) % X
        slot_core = (core + step) % 2
        slot = slot_x * 2 + slot_core

        @pl.when(step % 2 == 1)
        def _():
            arrived(stream.at[slot], core_recv.at[slot_x])

        rr = lax.broadcasted_iota(jnp.int32, (ROWS, CHUNK), 1)
        lane = lax.broadcasted_iota(jnp.int32, (ROWS, CHUNK), 0)
        pick = (lane == slot_x * PIECE + rr % PIECE).astype(jnp.bfloat16)
        spread = 64.0 * jnp.dot(high, pick, preferred_element_type=jnp.float32) + jnp.dot(
            low, pick, preferred_element_type=jnp.float32
        )
        rr = lax.broadcasted_iota(jnp.int32, (16, CHUNK), 1)
        source = lax.broadcasted_iota(jnp.int32, (16, CHUNK), 0)
        spread = jnp.where(source == (rr // PIECE) * 2 + slot_core, spread, 0.0)
        stream_place = jnp.sum(spread, axis=0, keepdims=True)
        stream_number = number(
            lax.broadcasted_iota(jnp.int32, (1, CHUNK), 1), slot_x, slot_core
        ).astype(jnp.float32)
        stream_key = jnp.where(side == 0, stream_number, stream_place)

        block = stream[slot]
        logits = heat * lax.dot_general(
            own[...], block, contract, preferred_element_type=jnp.float32
        ) + bias
        label = jnp.where(own_key == stream_key, 1.0, -1.0)
        weight = (
            -label * heat * jax.nn.sigmoid(-label * logits) / ROWS
        ).astype(jnp.bfloat16)
        total[...] += jnp.dot(weight, block, preferred_element_type=jnp.float32)

    result[...] = total[...].astype(jnp.bfloat16)
    owner = (group + side) % 32

    def give_back(step, act):
        at = (owner, step * 2 + core)
        act(
            result.at[rows(step)], landing.at[side, rows(x)],
            back_send.at[step], back_recv.at[side], at,
        )

    @pl.loop(0, 8)
    def _(step):
        give_back((z_lo + 4 + step) % 8, start)

    arrived(landing.at[0], back_recv.at[0])
    image_out[...] = landing[0].astype(jnp.float32)
    arrived(landing.at[1], back_recv.at[1])
    text_out[...] = landing[1].astype(jnp.float32)

    @pl.loop(0, X)
    def _(step):
        scatter(step, finish)

    @pl.loop(0, 16)
    def _(step):
        tell(step, finish)

    @pl.loop(0, LEVELS)
    def _(step):
        along_z(step, finish, False)

    @pl.loop(0, 8)
    def _(step):
        give_back(step, finish)

    @pl.loop(0, X)
    def _(step):
        copy(own, own, core_send.at[step], y_recv, twin).wait_send()

    copy(own, own, x_send.at[0], y_recv, to_right).wait_send()
    copy(own, own, x_send.at[1], y_recv, to_left).wait_send()
    copy(own, own, y_send, y_recv, across).wait_send()
    part = own.at[pl.ds(0, 4 * PIECE)]
    copy(part, part, far_send.at[0], y_recv, to_right).wait_send()
    copy(part, part, far_send.at[1], y_recv, to_left).wait_send()


def per_device(picture_embeddings, text_emb, positive, ln_inverse_heat, logit_bias):
    width = picture_embeddings.shape[1]
    vmem = pl.BlockSpec(memory_space=pltpu.VMEM)
    smem = pl.BlockSpec(memory_space=pltpu.SMEM)
    out = jax.ShapeDtypeStruct(picture_embeddings.shape, jnp.float32)
    dma = pltpu.SemaphoreType.DMA
    return pl.pallas_call(
        kernel,
        out_shape=(out, out),
        in_specs=[smem, smem, vmem, vmem, vmem],
        out_specs=(vmem, vmem),
        scratch_shapes=[
            pltpu.VMEM((CHUNK, width), jnp.bfloat16),
            pltpu.VMEM((8, CHUNK, width), jnp.bfloat16),
            pltpu.VMEM((CHUNK, width), jnp.bfloat16),
            pltpu.VMEM((CHUNK, width), jnp.float32),
            pltpu.VMEM((CHUNK, width), jnp.bfloat16),
            pltpu.VMEM((2, ROWS, width), jnp.bfloat16),
            pltpu.VMEM((16, ROWS), jnp.int32),
            dma((8,)), dma((8,)), dma((8,)), dma((8,)),
            dma((2,)), dma((8,)), dma((8,)), dma((2,)), dma((8,)),
            dma((4,)), dma((4,)), dma, dma, dma((8,)), dma((2,)), dma((16,)), dma,
        ],
        compiler_params=pltpu.CompilerParams(
            has_side_effects=True, vmem_limit_bytes=40 << 20
        ),
        cost_estimate=pl.CostEstimate(
            flops=4 * CHUNK * 2048 * width, bytes_accessed=8 << 20, transcendentals=CHUNK * 2048
        ),
        name="pair_blocks",
    )(ln_inverse_heat, logit_bias, picture_embeddings, text_emb, positive.reshape(1, ROWS))


def solution(mesh):
    spread = P(("outer", "inner"), None)
    return jax.shard_map(
        per_device,
        mesh=mesh,
        in_specs=(spread, spread, P(("outer", "inner")), P(), P()),
        out_specs=(spread, spread),
        check_vma=False,
    )
```

time: 378 us -> 162 us (0.43)
  the two profiles are of different devices: /device:TPU:1 before, /device:TPU:22 now
where the time goes in v1:
time: 162 us
  Pallas kernels  156 us (96%)
  local copies, waits for them, and re-layouts  4.4 us (3%)
  between operations  1.94 us (1%)
    pallas_call x1, Pallas kernels, per_device(): pl.pallas_call(kernel, out_shape=(out, out), in_specs=[smem, smem, vmem,...  156 us
    unnamed x8, local copies, waits for them, and re-layouts  4.4 us

profile of v1, /device:TPU:22, one launch (start us, length us, event | category | flops | bytes accessed | tf_op | source)
XLA Modules:
  0.0 162.2 jit_solution(16693021613623076939)
XLA Ops:
  1.9 0.0 copy-start.2
  1.9 0.6 copy-done.2
  2.6 0.0 copy-start
  2.6 1.0 copy-done
  3.6 0.0 copy-start.1
  3.6 1.0 copy-done.1
  4.6 155.8 %pair_blocks.1 = (f32[128,1536]{1,0:T(8,128)S(1)}, f32[128,1536]{1,0:T(8,128)S(1)}) custom-call(f32[1]{0:T(128)S(6)} %copy.9.heat_ref, f32[1]{0:T(128)S(6)} %copy.10.bias_ref, bf16[128,1536]{1,0:T(8,128)(2,1)S(1)} %copy-done, bf16[128,1536]{1,0:T(8,128)(2,1)S(1)} %copy-done.1, s32[1,128]{1,0:T(1,128)S(1)} %bitcast.1), custom_call_target="tpu_custom_call" | custom-call | flops 3221225472 | bytes 8388608 | tf_op jit(solution)/shard_map/pair_blocks/pallas_call | solution.py:288
  160.4 0.9 copy.11
  161.3 0.9 copy.12
Async XLA Ops:
  1.9 0.7 copy-start.2
  2.6 1.0 copy-start
  3.6 1.0 copy-start.1

commit v2 on v1

v2 whole, which is shorter than its diff:
```python
import jax
import jax.numpy as jnp
from jax import lax
from jax.experimental import pallas as pl
from jax.experimental.pallas import tpu as pltpu
from jax.sharding import PartitionSpec as P

X = 4
LEVELS = 16
PIECE = 32
ROWS = 128
HALF = 16
CHUNK = 256
HELD = 8
WINDOW = 4
LEAD = 16
LAG1, LAG2, LAG3 = 3, 6, 9
MESH = pl.DeviceIdType.MESH


def offset_of(step):
    return ((step + 1) // 2) * (2 * (step % 2) - 1)


def device(column, z, core):
    return (2 * column + z // 8, (z % 8) * 2 + core)


def rows(index, size=PIECE):
    return pl.ds(pl.multiple_of(index * size, size), size)


def kernel(
    heat_ref, bias_ref, image_ref, text_ref, positive_ref,
    image_out, text_out,
    relay, data, total, result, places,
    f1_send, f1_recv, f2_send, f2_recv, x_send, left_recv, right_recv, far_send, far_recv,
    core_send, core_recv, y_send, y_recv, back_send, back_recv, place_send, place_recv,
):
    outer, inner = lax.axis_index("outer"), lax.axis_index("inner")
    column, z_hi = outer // 2, outer % 2
    y, x = column // X, column % X
    z_lo, core = inner // 2, inner % 2
    z = z_hi * 8 + z_lo
    patch, side = y // 2, y % 2
    half = z % 2
    group = 2 * (patch * 8 + z // 2) + half
    mine = x * 2 + core
    before = (outer + 31) % 32

    def copy(source, target, send, receive, to):
        return pltpu.make_async_remote_copy(
            src_ref=source, dst_ref=target, send_sem=send, recv_sem=receive,
            device_id=to, device_id_type=MESH,
        )

    def start(source, target, send, receive, to):
        same = (to[0] == outer) & (to[1] == inner)

        @pl.when(same)
        def _():
            pltpu.make_async_copy(source, target, receive).start()

        @pl.when(jnp.logical_not(same))
        def _():
            copy(source, target, send, receive, to).start()

    def finish(source, target, send, receive, to):
        same = (to[0] == outer) & (to[1] == inner)

        @pl.when(jnp.logical_not(same))
        def _():
            copy(source, target, send, receive, to).wait_send()

    barrier = pltpu.get_barrier_semaphore()

    def greet(to):
        @pl.when((to[0] != outer) | (to[1] != inner))
        def _():
            pl.semaphore_signal(barrier, inc=1, device_id=to, device_id_type=MESH)

    to_right = (2 * (y * X + (x + 1) % X) + z_hi, inner)
    to_left = (2 * (y * X + (x + 3) % X) + z_hi, inner)
    across = (2 * ((y + 1 - 2 * side) * X + x) + z_hi, inner)
    twin = (outer, z_lo * 2 + 1 - core)

    @pl.loop(0, LEVELS)
    def _(step):
        kind = (step + z_hi) % 2
        greet(((2 * patch * 8 + step + kind) % 32, inner))
        greet(device(column, step, core))
        greet((group, step))

    @pl.loop(0, X)
    def _(step):
        greet(device(2 * patch * X + step, 2 * (column % 8) + z_hi, core))
        greet(device(
            (2 * (before // 16) + 1) * X + step, before % 16, core
        ))

    for to in (to_right, to_left, across, twin):
        pl.semaphore_signal(barrier, inc=1, device_id=to, device_id_type=MESH)
    owner = (group + side) % 32
    selves = (
        2
        + (before // 16 == patch).astype(jnp.int32)
        + (z == 2 * (column % 8) + z_hi).astype(jnp.int32)
        + (owner == outer).astype(jnp.int32)
    )
    pl.semaphore_wait(barrier, 60 - selves)

    def scatter(kind, act):
        ref = (image_ref, text_ref)[kind]
        his = (outer + 32 - kind) % 32
        level = his % 16

        @pl.loop(0, 8)
        def _(step):
            to = (2 * ((2 * (his // 16) + step % 2) * X + step // 2) + z_hi, inner)
            act(
                ref.at[rows(step, HALF)], relay.at[rows(level, HALF)],
                f1_send.at[kind * 8 + step], f1_recv.at[level], to,
            )

    def scatter_at(step, kind):
        level = (outer + 32 - kind) % 16
        ahead = (level - z + 7 + LEVELS) % LEVELS - 7
        turn = jnp.where(ahead > 0, 2 * ahead - 1, -2 * ahead)

        @pl.when(step == jnp.maximum(turn - LEAD, 0))
        def _():
            scatter(kind, start)

    def tell(step, act):
        q = column % 8
        target_column = (2 * patch + step // 8) * X + (step // 2) % X
        act(
            positive_ref, places.at[pl.ds(inner, 1)], place_send.at[step], place_recv,
            device(target_column, 2 * q + z_hi, step % 2),
        )

    @pl.loop(0, 16)
    def _(step):
        tell(step, start)

    def streams(from_half, level_half):
        return (from_half == level_half) == (side == 1)

    def along_z(step, act):
        level = (z + offset_of(step) + LEVELS) % LEVELS
        slot = jnp.where(streams(z_hi, level % 2), mine, HELD)
        act(
            relay.at[rows(level, HALF)], data.at[slot, rows(2 * z_lo + side, HALF)],
            f2_send.at[step], f2_recv.at[z], device(column, level, core),
        )

    def send_along_z(step):
        @pl.when(step < LEVELS)
        def _():
            level = (z + offset_of(step) + LEVELS) % LEVELS
            arrived(relay.at[rows(level, HALF)], f1_recv.at[level])

            @pl.when(step >= WINDOW)
            def _():
                along_z(step - WINDOW, finish)

            along_z(step, start)

    left, right, far = (x + 3) % X, (x + 1) % X, (x + 2) % X

    def arrived(ref, receive):
        copy(ref, ref, f1_send.at[0], receive, (outer, inner)).wait_recv()

    def at_step(step, act):
        @pl.when((step >= 0) & (step < LEVELS))
        def _():
            from_z = (z - offset_of(step) + LEVELS) % LEVELS
            act(from_z, from_z % 8, streams(from_z // 8, half))

    def from_level(from_z, zl, streaming):
        here = data.at[jnp.where(streaming, mine, HELD), rows(2 * zl + side, HALF)]
        arrived(here, f2_recv.at[from_z])
        there = data.at[jnp.where(streaming, HELD, mine), rows(2 * zl + side, HALF)]
        copy(here, there, y_send, y_recv.at[from_z], across).start()

    def from_across(from_z, zl, streaming):
        other = data.at[jnp.where(streaming, mine, HELD), rows(2 * zl + 1 - side, HALF)]
        arrived(other, y_recv.at[from_z])

        @pl.when(streaming)
        def _():
            here = data.at[mine, rows(zl)]
            copy(here, here, x_send.at[0], left_recv.at[zl], to_right).start()
            copy(here, here, x_send.at[1], right_recv.at[zl], to_left).start()
            copy(here, here, core_send.at[x], core_recv.at[x], twin).start()

    def from_sides(from_z, zl, streaming):
        @pl.when(streaming)
        def _():
            here = data.at[left * 2 + core, rows(zl)]
            arrived(here, left_recv.at[zl])

            @pl.when(zl % 2 == 0)
            def _():
                copy(here, here, far_send.at[0], far_recv.at[zl], to_right).start()

            copy(here, here, core_send.at[left], core_recv.at[left], twin).start()
            there = data.at[right * 2 + core, rows(zl)]
            arrived(there, right_recv.at[zl])

            @pl.when(zl % 2 == 1)
            def _():
                copy(there, there, far_send.at[1], far_recv.at[zl], to_left).start()

            copy(there, there, core_send.at[right], core_recv.at[right], twin).start()

    def from_far(from_z, zl, streaming):
        @pl.when(streaming)
        def _():
            here = data.at[far * 2 + core, rows(zl)]
            arrived(here, far_recv.at[zl])
            copy(here, here, core_send.at[far], core_recv.at[far], twin).start()

    @pl.loop(0, LEVELS + WINDOW + LAG3)
    def _(step):
        scatter_at(step, 0)
        scatter_at(step, 1)
        at_step(step - WINDOW - LAG3, from_far)
        at_step(step - WINDOW - LAG2, from_sides)
        at_step(step - WINDOW - LAG1, from_across)
        send_along_z(step)
        at_step(step - WINDOW, from_level)

    arrived(places, place_recv)
    place = (places[...] % 2048).astype(jnp.float32)
    high = jnp.floor(place * (1.0 / 64.0))
    low = (place - 64.0 * high).astype(jnp.bfloat16)
    high = high.astype(jnp.bfloat16)

    def number(rr, slot_x, slot_core):
        return ((rr // PIECE) * 2 + slot_core) * ROWS + slot_x * PIECE + rr % PIECE

    rr = lax.broadcasted_iota(jnp.int32, (CHUNK, ROWS), 0)
    lane = lax.broadcasted_iota(jnp.int32, (CHUNK, ROWS), 1)
    pick = (lane == x * PIECE + rr % PIECE).astype(jnp.bfloat16)
    contract = (((1,), (1,)), ((), ()))
    spread = 64.0 * lax.dot_general(
        pick, high, contract, preferred_element_type=jnp.float32
    ) + lax.dot_general(pick, low, contract, preferred_element_type=jnp.float32)
    rr = lax.broadcasted_iota(jnp.int32, (CHUNK, 16), 0)
    source = lax.broadcasted_iota(jnp.int32, (CHUNK, 16), 1)
    spread = jnp.where(source == (rr // PIECE) * 2 + core, spread, 0.0)
    own_place = jnp.sum(spread, axis=1, keepdims=True)
    own_number = number(
        lax.broadcasted_iota(jnp.int32, (CHUNK, 1), 0), x, core
    ).astype(jnp.float32)
    own_key = jnp.where(side == 0, own_place, own_number)

    heat = jnp.exp(jnp.full((1, CHUNK), heat_ref[0], jnp.float32))
    bias = bias_ref[0]
    total[...] = jnp.zeros_like(total)

    @pl.loop(0, 8)
    def _(step):
        turn = step // 2
        slot_x = (x + turn + turn // 2 - 2 * (turn // 3)) % X
        slot_core = (core + step) % 2
        slot = slot_x * 2 + slot_core

        @pl.when(step % 2 == 1)
        def _():
            arrived(data.at[slot], core_recv.at[slot_x])

        rr = lax.broadcasted_iota(jnp.int32, (ROWS, CHUNK), 1)
        lane = lax.broadcasted_iota(jnp.int32, (ROWS, CHUNK), 0)
        pick = (lane == slot_x * PIECE + rr % PIECE).astype(jnp.bfloat16)
        spread = 64.0 * jnp.dot(high, pick, preferred_element_type=jnp.float32) + jnp.dot(
            low, pick, preferred_element_type=jnp.float32
        )
        rr = lax.broadcasted_iota(jnp.int32, (16, CHUNK), 1)
        source = lax.broadcasted_iota(jnp.int32, (16, CHUNK), 0)
        spread = jnp.where(source == (rr // PIECE) * 2 + slot_core, spread, 0.0)
        stream_place = jnp.sum(spread, axis=0, keepdims=True)
        stream_number = number(
            lax.broadcasted_iota(jnp.int32, (1, CHUNK), 1), slot_x, slot_core
        ).astype(jnp.float32)
        stream_key = jnp.where(side == 0, stream_number, stream_place)

        block = data[slot]
        logits = heat * lax.dot_general(
            data[HELD], block, contract, preferred_element_type=jnp.float32
        ) + bias
        label = jnp.where(own_key == stream_key, 1.0, -1.0)
        weight = (
            -label * heat * jax.nn.sigmoid(-label * logits) / ROWS
        ).astype(jnp.bfloat16)
        total[...] += jnp.dot(weight, block, preferred_element_type=jnp.float32)

    result[...] = total[...].astype(jnp.bfloat16)

    def give_back(step, act):
        at = (owner, step * 2 + core)

        @pl.when(side == 0)
        def _():
            act(
                result.at[rows(step)], image_out.at[rows(x)],
                back_send.at[step], back_recv.at[0], at,
            )

        @pl.when(side == 1)
        def _():
            act(
                result.at[rows(step)], text_out.at[rows(x)],
                back_send.at[step], back_recv.at[1], at,
            )

    @pl.loop(0, 8)
    def _(step):
        give_back((z_lo + step) % 8, start)

    arrived(image_out, back_recv.at[0])
    arrived(text_out, back_recv.at[1])

    scatter(0, finish)
    scatter(1, finish)

    @pl.loop(0, 16)
    def _(step):
        tell(step, finish)

    @pl.loop(LEVELS - WINDOW, LEVELS)
    def _(step):
        along_z(step, finish)

    @pl.loop(0, 8)
    def _(step):
        give_back(step, finish)

    whole = data.at[HELD]

    @pl.loop(0, X)
    def _(step):
        copy(whole, whole, core_send.at[step], place_recv, twin).wait_send()

    copy(whole, whole, y_send, place_recv, across).wait_send()
    part = data.at[HELD, pl.ds(0, CHUNK // 2)]
    for step, to in enumerate((to_right, to_left)):
        copy(whole, whole, x_send.at[step], place_recv, to).wait_send()
        copy(part, part, far_send.at[step], place_recv, to).wait_send()


def per_device(picture_embeddings, text_emb, positive, ln_inverse_heat, logit_bias):
    width = picture_embeddings.shape[1]
    anywhere = pl.BlockSpec(memory_space=pl.ANY)
    hbm = pl.BlockSpec(memory_space=pltpu.HBM)
    smem = pl.BlockSpec(memory_space=pltpu.SMEM)
    out = jax.ShapeDtypeStruct(picture_embeddings.shape, jnp.bfloat16)
    dma = pltpu.SemaphoreType.DMA
    image_grad, text_grad = pl.pallas_call(
        kernel,
        out_shape=(out, out),
        in_specs=[smem, smem, hbm, hbm, hbm],
        out_specs=(anywhere, anywhere),
        scratch_shapes=[
            pltpu.VMEM((LEVELS * HALF, width), jnp.bfloat16),
            pltpu.VMEM((HELD + 1, CHUNK, width), jnp.bfloat16),
            pltpu.VMEM((CHUNK, width), jnp.float32),
            pltpu.VMEM((CHUNK, width), jnp.bfloat16),
            pltpu.VMEM((16, ROWS), jnp.int32),
            dma((16,)), dma((16,)), dma((16,)), dma((16,)),
            dma((2,)), dma((8,)), dma((8,)), dma((2,)), dma((8,)),
            dma((4,)), dma((4,)), dma, dma((16,)), dma((8,)), dma((2,)), dma((16,)), dma,
        ],
        compiler_params=pltpu.CompilerParams(
            collective_id=0, has_side_effects=True, vmem_limit_bytes=40 << 20
        ),
        cost_estimate=pl.CostEstimate(
            flops=4 * CHUNK * 2048 * width, bytes_accessed=8 << 20, transcendentals=CHUNK * 2048
        ),
        name="pair_blocks",
    )(ln_inverse_heat, logit_bias, picture_embeddings, text_emb, positive.reshape(1, ROWS))
    return image_grad.astype(jnp.float32), text_grad.astype(jnp.float32)


def solution(mesh):
    spread = P(("outer", "inner"), None)
    return jax.shard_map(
        per_device,
        mesh=mesh,
        in_specs=(spread, spread, P(("outer", "inner")), P(), P()),
        out_specs=(spread, spread),
        check_vma=False,
    )
```

time: 162 us -> 128 us (0.79)
  the two profiles are of different devices: /device:TPU:22 before, /device:TPU:504 now
where the time goes in v2:
time: 128 us; the launch traced here: 126 us
  Pallas kernels  120 us (94%)
  local copies, waits for them, and re-layouts  2.64 us (2%)
  between operations  1.94 us (2%)
  other arithmetic  1.92 us (2%)
    pallas_call x1, Pallas kernels, per_device(): pl.pallas_call(kernel, out_shape=(out, out), in_specs=[smem, smem, hbm, h...  120 us
    unnamed x6, local copies, waits for them, and re-layouts  2.64 us

profile of v2, /device:TPU:504, one launch (start us, length us, event | category | flops | bytes accessed | tf_op | source)
XLA Modules:
  0.0 126.1 jit_solution(5104853522438082876)
XLA Ops:
  1.9 0.0 copy-start.2
  1.9 0.6 copy-done.2
  2.6 0.0 copy-start
  2.6 1.0 copy-done
  3.6 0.0 copy-start.1
  3.6 1.0 copy-done.1
  4.6 119.6 %pair_blocks.1 = (bf16[128,1536]{1,0:T(8,128)(2,1)S(1)}, bf16[128,1536]{1,0:T(8,128)(2,1)S(1)}) custom-call(f32[1]{0:T(128)S(6)} %copy.7.heat_ref, f32[1]{0:T(128)S(6)} %copy.8.bias_ref, bf16[128,1536]{1,0:T(8,128)(2,1)S(1)} %copy-done, bf16[128,1536]{1,0:T(8,128)(2,1)S(1)} %copy-done.1, s32[1,128]{1,0:T(1,128)S(1)} %bitcast.1), custom_call_target="tpu_custom_call" | custom-call | flops 3221225472 | bytes 8388608 | tf_op jit(solution)/shard_map/pair_blocks/pallas_call | solution.py:360
  124.2 1.0 convert_element_type.6
  125.2 1.0 convert_element_type.7
Async XLA Ops:
  1.9 0.7 copy-start.2
  2.6 1.0 copy-start
  3.6 1.0 copy-start.1

commit v3 on v2

--- a/solution.py
+++ b/solution.py
@@ -31,8 +31,9 @@
 
 
 def kernel(
-    heat_ref, bias_ref, image_ref, text_ref, positive_ref,
+    heat_ref, bias_ref, image_in, text_in, positive_in,
     image_out, text_out,
+    image_ref, text_ref, positive_ref, load_sem,
     relay, data, total, result, places,
     f1_send, f1_recv, f2_send, f2_recv, x_send, left_recv, right_recv, far_send, far_recv,
     core_send, core_recv, y_send, y_recv, back_send, back_recv, place_send, place_recv,
@@ -72,6 +73,15 @@
         def _():
             copy(source, target, send, receive, to).wait_send()
 
+    loads = [
+        pltpu.make_async_copy(source, target, load_sem.at[index])
+        for index, (source, target) in enumerate(
+            ((image_in, image_ref), (text_in, text_ref), (positive_in, positive_ref))
+        )
+    ]
+    for load in loads:
+        load.start()
+
     barrier = pltpu.get_barrier_semaphore()
 
     def greet(to):
@@ -108,6 +118,8 @@
         + (owner == outer).astype(jnp.int32)
     )
     pl.semaphore_wait(barrier, 60 - selves)
+    for load in loads:
+        load.wait()
 
     def scatter(kind, act):
         ref = (image_ref, text_ref)[kind]
@@ -363,6 +375,10 @@
         in_specs=[smem, smem, hbm, hbm, hbm],
         out_specs=(anywhere, anywhere),
         scratch_shapes=[
+            pltpu.VMEM((ROWS, width), jnp.bfloat16),
+            pltpu.VMEM((ROWS, width), jnp.bfloat16),
+            pltpu.VMEM((1, ROWS), jnp.int32),
+            dma((3,)),
             pltpu.VMEM((LEVELS * HALF, width), jnp.bfloat16),
             pltpu.VMEM((HELD + 1, CHUNK, width), jnp.bfloat16),
             pltpu.VMEM((CHUNK, width), jnp.float32),
@@ -373,7 +389,7 @@
             dma((4,)), dma((4,)), dma, dma((16,)), dma((8,)), dma((2,)), dma((16,)), dma,
         ],
         compiler_params=pltpu.CompilerParams(
-            collective_id=0, has_side_effects=True, vmem_limit_bytes=40 << 20
+            collective_id=0, has_side_effects=True, vmem_limit_bytes=60 << 20
         ),
         cost_estimate=pl.CostEstimate(
             flops=4 * CHUNK * 2048 * width, bytes_accessed=8 << 20, transcendentals=CHUNK * 2048

time: 128 us -> 127 us (level); the launches traced: 126 us -> 127 us
  local copies, waits for them, and re-layouts: 2.64 us -> 0.01 us
  Pallas kernels: 120 us -> 122 us
    unnamed x6 -> x2, local copies, waits for them, and re-layouts: 2.64 us -> 0.01 us
    pallas_call x1, Pallas kernels: 120 us -> 122 us  [per_device(): pl.pallas_call(kernel, out_shape=(out, out), in_specs=[smem, smem, hbm, h...]
where the time goes in v3:
time: 127 us
  Pallas kernels  122 us (96%)
  other arithmetic  2.96 us (2%)
  between operations  1.94 us (2%)
    pallas_call x1, Pallas kernels, per_device(): pl.pallas_call(kernel, out_shape=(out, out), in_specs=[smem, smem, hbm, h...  122 us
    convert_element_type x2, other arithmetic, per_device(): return (image_grad.astype(jnp.float32), text_grad.astype(jnp.float32))  2.96 us

profile of v3, /device:TPU:504, one launch (start us, length us, event | category | flops | bytes accessed | tf_op | source)
XLA Modules:
  0.0 126.8 jit_solution(16111499941947029317)
XLA Ops:
  1.9 121.9 %pair_blocks.1 = (bf16[128,1536]{1,0:T(8,128)(2,1)}, bf16[128,1536]{1,0:T(8,128)(2,1)}) custom-call(f32[1]{0:T(128)S(6)} %copy.7.heat_ref, f32[1]{0:T(128)S(6)} %copy.8.bias_ref, bf16[128,1536]{1,0:T(8,128)(2,1)} %image_in.1, bf16[128,1536]{1,0:T(8,128)(2,1)} %text_in.1, s32[1,128]{1,0:T(1,128)} %bitcast.1), custom_call_target="tpu_custom_call" | custom-call | flops 3221225472 | bytes 8388608 | tf_op jit(solution)/shard_map/pair_blocks/pallas_call | solution.py:372
  123.9 0.0 copy-start
  123.9 2.0 %convert_element_type.6 = f32[128,1536]{1,0:T(8,128)} convert(bf16[128,1536]{1,0:T(8,128)(2,1)} %get-tuple-element.4) | non-fusion elementwise | flops 196608 | bytes 1179648 | tf_op jit(solution)/shard_map/convert_element_type | solution.py:399
  125.9 0.0 copy-done
  125.9 1.0 convert_element_type.7
Async XLA Ops:
  123.9 2.0 %copy-start = (bf16[128,1536]{1,0:T(8,128)(2,1)S(1)}, bf16[128,1536]{1,0:T(8,128)(2,1)}, u32[]{:S(2)}) copy-start(bf16[128,1536]{1,0:T(8,128)(2,1)} %get-tuple-element.5) | copy-start | bytes 1179652

commit v4 on v3

--- a/solution.py
+++ b/solution.py
@@ -329,7 +329,8 @@
 
     @pl.loop(0, 8)
     def _(step):
-        give_back((z_lo + step) % 8, start)
+        across_ring = jnp.where(owner % 2 == z_hi, 0, 4)
+        give_back((z_lo + across_ring + step) % 8, start)
 
     arrived(image_out, back_recv.at[0])
     arrived(text_out, back_recv.at[1])

time: 127 us -> 127 us (level)
  no operation moved by 1% of the time
where the time goes in v4:
time: 127 us; the launch traced here: 126 us
  Pallas kernels  121 us (95%)
  other arithmetic  2.96 us (2%)
  between operations  1.94 us (2%)
    pallas_call x1, Pallas kernels, per_device(): pl.pallas_call(kernel, out_shape=(out, out), in_specs=[smem, smem, hbm, h...  121 us
    convert_element_type x2, other arithmetic, per_device(): return (image_grad.astype(jnp.float32), text_grad.astype(jnp.float32))  2.96 us

profile of v4, /device:TPU:504, one launch (start us, length us, event | category | flops | bytes accessed | tf_op | source)
XLA Modules:
  0.0 125.7 jit_solution(12884931324758990475)
XLA Ops:
  1.9 120.8 %pair_blocks.1 = (bf16[128,1536]{1,0:T(8,128)(2,1)}, bf16[128,1536]{1,0:T(8,128)(2,1)}) custom-call(f32[1]{0:T(128)S(6)} %copy.7.heat_ref, f32[1]{0:T(128)S(6)} %copy.8.bias_ref, bf16[128,1536]{1,0:T(8,128)(2,1)} %image_in.1, bf16[128,1536]{1,0:T(8,128)(2,1)} %text_in.1, s32[1,128]{1,0:T(1,128)} %bitcast.1), custom_call_target="tpu_custom_call" | custom-call | flops 3221225472 | bytes 8388608 | tf_op jit(solution)/shard_map/pair_blocks/pallas_call | solution.py:373
  122.7 0.0 copy-start
  122.7 2.0 %convert_element_type.6 = f32[128,1536]{1,0:T(8,128)} convert(bf16[128,1536]{1,0:T(8,128)(2,1)} %get-tuple-element.4) | non-fusion elementwise | flops 196608 | bytes 1179648 | tf_op jit(solution)/shard_map/convert_element_type | solution.py:400
  124.7 0.0 copy-done
  124.7 1.0 convert_element_type.7
Async XLA Ops:
  122.7 2.0 %copy-start = (bf16[128,1536]{1,0:T(8,128)(2,1)S(1)}, bf16[128,1536]{1,0:T(8,128)(2,1)}, u32[]{:S(2)}) copy-start(bf16[128,1536]{1,0:T(8,128)(2,1)} %get-tuple-element.5) | copy-start | bytes 1179652
